TPU v7x, 32 devices: a whole 2x2x4 slice. The times are simulated.
32 devices in a mesh: site: 4 (over x, core), sec: 8 (over z, y).
Axes of the slice: x: 2, y: 2, z: 4, core: 2. Of those that a mesh axis runs over, the one named last changes fastest.
Arguments:
- tensors: bfloat16 [4, 16, 4, 512, 512], P('site', 'sec'), as said below
- factors: float32 [4, 16, 512, 512], P('site', 'sec'), as said below
- sector_sizes: int32 [4, 16], replicated, may hold values from 384 to 512, as said below
- merging: int32 [4, 16, 4], replicated, may hold values from 0 to 15, as said below
Outputs:
- isometry: float32 [4, 16, 4, 512, 512], P('site', 'sec')
- factor_out: float32 [4, 16, 512, 512], P('site', 'sec')
Inputs may be any that keep to these rules, and one draw needn't show every extreme that they name: `sector_sizes`: every bond has one sector of exactly 512 states and one of exactly 384. For every site and physical state, merging maps the left sectors one to one onto the right sectors; the 8 blocks (left sector, physical state) of the left sectors that lie on one index of sec go to 8 different indices of sec, one block to each. `tensors`: zero outside the rows below the left sector's size and the columns below the right sector's size. `factors`: upper triangular with a positive diagonal inside the sector's size, the identity on its padding.
All inputs are finite; a program needn't handle non-finite values.
Results may differ from a plain program's by a relative error of at most 0.007.
Values may be sent and summed in bfloat16 or wider, within the bound.
A program may use at most 192 MiB of HBM per device.

v0:
```python
import math

import jax
import jax.numpy as jnp
from jax import lax
from jax.sharding import PartitionSpec as P

ROUNDS = 3


def from_behind(shard, axis, by):
    size = lax.axis_size(axis)
    return lax.ppermute(shard, axis, [(i, (i + by) % size) for i in range(size)])


def routing_maps(merging_rows, sec_index, sec_groups, sec_local, phys_count):
    total_keys = sec_groups * sec_local * phys_count
    ordinal = jnp.arange(total_keys, dtype=jnp.int32)
    left_sector = ordinal // phys_count
    phys_index = ordinal % phys_count
    right_sector = merging_rows.reshape(total_keys)
    source = left_sector // sec_local
    target = right_sector // sec_local
    local_count = sec_local * phys_count
    peers = jnp.arange(sec_groups, dtype=jnp.int32)
    own_targets = lax.dynamic_slice_in_dim(target, sec_index * local_count, local_count)
    send_map = (peers[:, None] == own_targets[None, :]).astype(jnp.bfloat16)
    row_id = jnp.where(
        target == sec_index, (right_sector - sec_index * sec_local) * phys_count + phys_index, -1
    )
    wanted = (jnp.arange(local_count, dtype=jnp.int32)[:, None] == row_id[None, :]).astype(
        jnp.float32
    )
    placed = (source[:, None] == peers[None, :]).astype(jnp.float32)
    pick_map = jnp.dot(wanted, placed, preferred_element_type=jnp.float32).astype(jnp.bfloat16)
    return (send_map, pick_map)


def send_blocks(flattened, send_map):
    return jnp.dot(send_map, flattened, preferred_element_type=jnp.float32).astype(jnp.bfloat16)


def pick_blocks(received, pick_map):
    return jnp.dot(pick_map, received, preferred_element_type=jnp.float32).astype(jnp.bfloat16)


def route_products(products, send_map, pick_map):
    outgoing = send_blocks(products, send_map)
    received = lax.all_to_all(outgoing, "sec", split_axis=0, concat_axis=0, tiled=True)
    return pick_blocks(received, pick_map)


def body(tensors, factors, sector_sizes, merging):
    site_index = lax.axis_index("site")
    sec_index = lax.axis_index("sec")
    site_count = lax.axis_size("site")
    sec_groups = lax.axis_size("sec")
    blocks = tensors[0]
    sec_local, phys_count, block_size = (blocks.shape[0], blocks.shape[1], blocks.shape[3])
    local_count = sec_local * phys_count
    block_area = block_size * block_size
    merging_rows = lax.dynamic_index_in_dim(merging, site_index, 0, keepdims=False)
    next_widths = lax.dynamic_index_in_dim(
        sector_sizes, (site_index + 1) % site_count, 0, keepdims=False
    )
    widths = lax.dynamic_slice_in_dim(next_widths, sec_index * sec_local, sec_local)
    padding = (jnp.arange(block_size, dtype=jnp.int32)[None, :] >= widths[:, None]).astype(
        jnp.float32
    )
    identity = jnp.eye(block_size, dtype=jnp.float32)
    send_map, pick_map = routing_maps(merging_rows, sec_index, sec_groups, sec_local, phys_count)
    carried = factors[0]
    for step_index in range(ROUNDS):
        left_factor = carried.astype(jnp.bfloat16)
        products = jnp.einsum(
            "ajk,apkl->apjl", left_factor, blocks, preferred_element_type=jnp.float32
        ).astype(jnp.bfloat16)
        stacked = route_products(products.reshape(local_count, block_area), send_map, pick_map)
        stacked = stacked.reshape(sec_local, phys_count * block_size, block_size)
        gram_matrix = jnp.einsum(
            "brl,brm->blm", stacked, stacked, preferred_element_type=jnp.float32
        )
        gram_matrix = gram_matrix + identity[None] * padding[:, None, :]
        lower_factor = jnp.linalg.cholesky(gram_matrix)
        upper_factor = jnp.swapaxes(lower_factor, -1, -2)
        if step_index + 1 < ROUNDS:
            outgoing_factor = upper_factor.astype(jnp.bfloat16)
            carried = from_behind(outgoing_factor, "site", 1)
    solved = lax.linalg.triangular_solve(
        lower_factor, stacked.astype(jnp.float32), left_side=False, lower=True, transpose_a=True
    )
    isometry = (solved * math.sqrt(phys_count * block_size)).reshape(
        1, sec_local, phys_count, block_size, block_size
    )
    return (isometry, upper_factor[None])


def solution(mesh):
    in_specs = (P("site", "sec", None, None, None), P("site", "sec", None, None), P(), P())
    out_specs = (P("site", "sec", None, None, None), P("site", "sec", None, None))
    return jax.shard_map(body, mesh=mesh, in_specs=in_specs, out_specs=out_specs, check_vma=False)
```

profile of v0, /device:TPU:0, one launch (start us, length us, event | category | flops | bytes accessed | tf_op | source)
XLA Modules:
  0.0 1145.3 jit_solution(17635938718964072204)
XLA Ops:
  1.5 7.9 convert_bitcast_fusion
  9.4 7.5 copy.165
  16.9 6.5 copy.251
  29.5 6.4 reduce.16
  35.9 8.1 reshape.271
  43.9 7.6 all-to-all-start
  52.9 91.9 %all-to-all-done = bf16[8,2,131072]{2,1,0:T(2,128)(2,1)} async-done(((bf16[8,2,131072]{2,1,0:T(2,128)(2,1)}), bf16[8,2,131072]{2,1,0:T(2,128)(2,1)}, u32[]{:S(2)}, u32[]{:S(2)}) %all-to-all-start) | async-done | bytes 4194336 | tf_op jit(solution)/shard_map/all_to_all | solution.py:49
  144.7 8.7 reshape.272
  153.5 10.1 convolution_convert_fusion.4
  180.8 23.9 %custom-call.42 = f32[2,128,128]{2,1,0:T(8,128)S(1)} custom-call(f32[2,128,128]{2,1,0:T(8,128)S(1)} %cholesky.586), custom_call_target="Cholesky" | custom-call | tf_op jit(solution)/shard_map/jit(cholesky)/cholesky | solution.py:84
  204.8 19.7 %custom-call.43 = f32[2,1,128,128]{2,3,1,0:T(8,128)S(1)} custom-call(f32[2,1,128,128]{3,2,1,0:T(8,128)S(1)} %select_bitcast_fusion.8), custom_call_target="InvertDiagBlocksLowerTriangular" | custom-call | tf_op jit(solution)/shard_map/jit(cholesky)/cholesky | solution.py:84
  227.7 23.5 %custom-call.44 = f32[2,128,128]{2,1,0:T(8,128)S(1)} custom-call(f32[2,128,128]{2,1,0:T(8,128)S(1)} %cholesky.590), custom_call_target="Cholesky" | custom-call | tf_op jit(solution)/shard_map/jit(cholesky)/cholesky | solution.py:84
  251.2 19.8 %custom-call.45 = f32[2,1,128,128]{2,3,1,0:T(8,128)S(1)} custom-call(f32[2,1,128,128]{3,2,1,0:T(8,128)S(1)} %get-tuple-element.60), custom_call_target="InvertDiagBlocksLowerTriangular" | custom-call | tf_op jit(solution)/shard_map/jit(cholesky)/cholesky | solution.py:84
  273.0 23.5 %custom-call.46 = f32[2,128,128]{2,1,0:T(8,128)S(1)} custom-call(f32[2,128,128]{2,1,0:T(8,128)S(1)} %cholesky.595), custom_call_target="Cholesky" | custom-call | tf_op jit(solution)/shard_map/jit(cholesky)/cholesky | solution.py:84
  296.5 19.7 %custom-call.47 = f32[2,1,128,128]{2,3,1,0:T(8,128)S(1)} custom-call(f32[2,1,128,128]{3,2,1,0:T(8,128)S(1)} %get-tuple-element.58), custom_call_target="InvertDiagBlocksLowerTriangular" | custom-call | tf_op jit(solution)/shard_map/jit(cholesky)/cholesky | solution.py:84
  318.0 23.7 %custom-call.48 = f32[2,128,128]{2,1,0:T(8,128)S(1)} custom-call(f32[2,128,128]{2,1,0:T(8,128)S(1)} %convolution_subtract_fusion.9), custom_call_target="Cholesky" | custom-call | tf_op jit(solution)/shard_map/jit(cholesky)/cholesky | solution.py:84
  342.6 14.2 %collective-permute-done = bf16[2,512,512]{1,2,0:T(8,128)(2,1)S(1)} collective-permute-done((bf16[2,512,512]{1,2,0:T(8,128)(2,1)S(1)}, bf16[2,512,512]{1,2,0:T(8,128)(2,1)S(1)}, u32[]{:S(2)}, u32[]{:S(2)}) %collective-permute-start) | collective-permute-done | bytes 1048608 | tf_op jit(solution)/shard_map/ppermute | solution.py:13
  367.0 6.8 reduce.17
  373.7 8.1 reshape.273
  381.8 97.4 %all_to_all.36 = bf16[8,2,131072]{2,1,0:T(2,128)(2,1)} all-to-all(bf16[8,2,131072]{2,1,0:T(2,128)(2,1)} %reshape.273), channel_id=1, replica_groups=mesh['site'=4,'sec'=8] {'sec'}, dimensions={0} | all-to-all | bytes 8388608 | tf_op jit(solution)/shard_map/all_to_all | solution.py:49
  479.3 8.7 reshape.274
  488.0 10.1 convolution_convert_fusion.2
  498.1 6.2 reshape.244
  515.4 23.6 %custom-call.49 = f32[2,128,128]{2,1,0:T(8,128)S(1)} custom-call(f32[2,128,128]{2,1,0:T(8,128)S(1)} %cholesky.599), custom_call_target="Cholesky" | custom-call | tf_op jit(solution)/shard_map/jit(cholesky)/cholesky | solution.py:84
  539.3 19.7 %custom-call.50 = f32[2,1,128,128]{2,3,1,0:T(8,128)S(1)} custom-call(f32[2,1,128,128]{3,2,1,0:T(8,128)S(1)} %select_bitcast_fusion.5), custom_call_target="InvertDiagBlocksLowerTriangular" | custom-call | tf_op jit(solution)/shard_map/jit(cholesky)/cholesky | solution.py:84
  562.1 23.5 %custom-call.51 = f32[2,128,128]{2,1,0:T(8,128)S(1)} custom-call(f32[2,128,128]{2,1,0:T(8,128)S(1)} %cholesky.603), custom_call_target="Cholesky" | custom-call | tf_op jit(solution)/shard_map/jit(cholesky)/cholesky | solution.py:84
  585.5 19.9 %custom-call.52 = f32[2,1,128,128]{2,3,1,0:T(8,128)S(1)} custom-call(f32[2,1,128,128]{3,2,1,0:T(8,128)S(1)} %get-tuple-element.55), custom_call_target="InvertDiagBlocksLowerTriangular" | custom-call | tf_op jit(solution)/shard_map/jit(cholesky)/cholesky | solution.py:84
  607.4 23.5 %custom-call.53 = f32[2,128,128]{2,1,0:T(8,128)S(1)} custom-call(f32[2,128,128]{2,1,0:T(8,128)S(1)} %cholesky.608), custom_call_target="Cholesky" | custom-call | tf_op jit(solution)/shard_map/jit(cholesky)/cholesky | solution.py:84
  630.9 19.7 %custom-call.54 = f32[2,1,128,128]{2,3,1,0:T(8,128)S(1)} custom-call(f32[2,1,128,128]{3,2,1,0:T(8,128)S(1)} %get-tuple-element.53), custom_call_target="InvertDiagBlocksLowerTriangular" | custom-call | tf_op jit(solution)/shard_map/jit(cholesky)/cholesky | solution.py:84
  652.4 23.9 %custom-call.55 = f32[2,128,128]{2,1,0:T(8,128)S(1)} custom-call(f32[2,128,128]{2,1,0:T(8,128)S(1)} %convolution_subtract_fusion.8), custom_call_target="Cholesky" | custom-call | tf_op jit(solution)/shard_map/jit(cholesky)/cholesky | solution.py:84
  677.4 14.2 %collective-permute-done.1 = bf16[2,512,512]{1,2,0:T(8,128)(2,1)S(1)} collective-permute-done((bf16[2,512,512]{1,2,0:T(8,128)(2,1)S(1)}, bf16[2,512,512]{1,2,0:T(8,128)(2,1)S(1)}, u32[]{:S(2)}, u32[]{:S(2)}) %collective-permute-start.1) | collective-permute-done | bytes 1048608 | tf_op jit(solution)/shard_map/ppermute | solution.py:13
  701.7 6.5 reduce.18
  708.2 8.1 reshape.275
  720.9 91.5 %all-to-all-done.2 = bf16[8,2,131072]{2,1,0:T(2,128)(2,1)} async-done(((bf16[8,2,131072]{2,1,0:T(2,128)(2,1)}), bf16[8,2,131072]{2,1,0:T(2,128)(2,1)}, u32[]{:S(2)}, u32[]{:S(2)}) %all-to-all-start.2) | async-done | bytes 4194336 | tf_op jit(solution)/shard_map/all_to_all | solution.py:49
  812.5 8.7 reshape.276
  821.2 10.1 convolution_convert_fusion
  831.3 6.1 reshape.246
  848.6 23.9 %custom-call.56 = f32[2,128,128]{2,1,0:T(8,128)S(1)} custom-call(f32[2,128,128]{2,1,0:T(8,128)S(1)} %cholesky.612), custom_call_target="Cholesky" | custom-call | tf_op jit(solution)/shard_map/jit(cholesky)/cholesky | solution.py:84
  872.7 6.8 convert_element_type.98
  879.5 19.7 %custom-call.57 = f32[2,1,128,128]{2,3,1,0:T(8,128)S(1)} custom-call(f32[2,1,128,128]{3,2,1,0:T(8,128)S(1)} %select_bitcast_fusion.2), custom_call_target="InvertDiagBlocksLowerTriangular" | custom-call | tf_op jit(solution)/shard_map/jit(cholesky)/cholesky | solution.py:84
  902.2 23.5 %custom-call.58 = f32[2,128,128]{2,1,0:T(8,128)S(1)} custom-call(f32[2,128,128]{2,1,0:T(8,128)S(1)} %cholesky.616), custom_call_target="Cholesky" | custom-call | tf_op jit(solution)/shard_map/jit(cholesky)/cholesky | solution.py:84
  925.7 19.8 %custom-call.59 = f32[2,1,128,128]{2,3,1,0:T(8,128)S(1)} custom-call(f32[2,1,128,128]{3,2,1,0:T(8,128)S(1)} %get-tuple-element.50), custom_call_target="InvertDiagBlocksLowerTriangular" | custom-call | tf_op jit(solution)/shard_map/jit(cholesky)/cholesky | solution.py:84
  947.5 23.5 %custom-call.60 = f32[2,128,128]{2,1,0:T(8,128)S(1)} custom-call(f32[2,128,128]{2,1,0:T(8,128)S(1)} %cholesky.621), custom_call_target="Cholesky" | custom-call | tf_op jit(solution)/shard_map/jit(cholesky)/cholesky | solution.py:84
  971.0 19.7 %custom-call.61 = f32[2,1,128,128]{2,3,1,0:T(8,128)S(1)} custom-call(f32[2,1,128,128]{3,2,1,0:T(8,128)S(1)} %get-tuple-element.48), custom_call_target="InvertDiagBlocksLowerTriangular" | custom-call | tf_op jit(solution)/shard_map/jit(cholesky)/cholesky | solution.py:84
  992.5 23.5 %custom-call.62 = f32[2,128,128]{2,1,0:T(8,128)S(1)} custom-call(f32[2,128,128]{2,1,0:T(8,128)S(1)} %convolution_subtract_fusion.7), custom_call_target="Cholesky" | custom-call | tf_op jit(solution)/shard_map/jit(cholesky)/cholesky | solution.py:84
  1022.1 14.1 %while.1 = (s32[]{:T(128)}, f32[2,512,512]{2,1,0:T(8,128)}, s32[4,2]{0,1:T(2,128)S(1)}, f32[4,2,128,128]{3,2,0,1:T(8,128)}, s32[]{:T(128)}) while((s32[]{:T(128)}, f32[2,512,512]{2,1,0:T(8,128)}, s32[4,2]{0,1:T(2,128)S(1)}, f32[4,2,128,128]{3,2,0,1:T(8,128)}, s32[]{:T(128)}) %tuple.54), condition=%wide.while_cond, body=%wide.while_body.sunk | while | flops 2 | bytes 263277 | solution.py:89
  1036.2 79.6 %custom-call.27 = f32[2,4,128,128]{2,3,1,0:T(8,128)S(1)} custom-call(f32[2,4,128,128]{3,2,1,0:T(8,128)} %bitcast.206), custom_call_target="InvertDiagBlocksLowerTriangular" | custom-call | tf_op jit(solution)/shard_map/triangular_solve | solution.py:89
  1131.0 8.0 fusion.36
  (131 shorter events, 136.8 us)
Async XLA Ops:
  0.6 0.7 copy-start
  43.9 100.8 %all-to-all-start = ((bf16[8,2,131072]{2,1,0:T(2,128)(2,1)}), bf16[8,2,131072]{2,1,0:T(2,128)(2,1)}, u32[]{:S(2)}, u32[]{:S(2)}) async-start(bf16[8,2,131072]{2,1,0:T(2,128)(2,1)} %reshape.271), calls=%async_computation | async-start | bytes 8388608 | tf_op jit(solution)/shard_map/all_to_all | solution.py:49
  52.6 117.1 %copy-start.5 = (f32[512,512]{0,1:T(8,128)}, f32[512,512]{0,1:T(8,128)S(1)}, u32[]{:S(2)}) copy-start(f32[512,512]{0,1:T(8,128)S(1)} %fusion.52) | copy-start | bytes 3145732
  179.5 1.3 copy-start.3
  342.5 14.3 %collective-permute-start = (bf16[2,512,512]{1,2,0:T(8,128)(2,1)S(1)}, bf16[2,512,512]{1,2,0:T(8,128)(2,1)S(1)}, u32[]{:S(2)}, u32[]{:S(2)}) collective-permute-start(bf16[2,512,512]{1,2,0:T(8,128)(2,1)S(1)} %fusion.44), channel_id=1, source_target_pairs={{0,8},{8,16},{16,24},{24,0},{1,9},{9,17},{17,25},{25,1},{2,10},{10... | collective-permute-start | bytes 3145736 | tf_op jit(solution)/shard_map/ppermute | solution.py:13
  498.1 6.2 copy-start.6
  514.1 1.3 copy-start.4
  677.3 14.3 %collective-permute-start.1 = (bf16[2,512,512]{1,2,0:T(8,128)(2,1)S(1)}, bf16[2,512,512]{1,2,0:T(8,128)(2,1)S(1)}, u32[]{:S(2)}, u32[]{:S(2)}) collective-permute-start(bf16[2,512,512]{1,2,0:T(8,128)(2,1)S(1)} %fusion.45), channel_id=1, source_target_pairs={{0,8},{8,16},{16,24},{24,0},{1,9},{9,17},{17,25},{25,1},{2,10},{10... | collective-permute-start | bytes 3145736 | tf_op jit(solution)/shard_map/ppermute | solution.py:13
  716.3 96.1 %all-to-all-start.2 = ((bf16[8,2,131072]{2,1,0:T(2,128)(2,1)}), bf16[8,2,131072]{2,1,0:T(2,128)(2,1)}, u32[]{:S(2)}, u32[]{:S(2)}) async-start(bf16[8,2,131072]{2,1,0:T(2,128)(2,1)} %reshape.275), calls=%async_computation.2 | async-start | bytes 8388608 | tf_op jit(solution)/shard_map/all_to_all | solution.py:49
  831.3 6.1 copy-start.7
  847.2 1.3 copy-start.2
  1140.8 4.1 copy-start.1
where the time goes:
time: 1150 us
  other arithmetic  583 us (51%)
  waiting for transfers between devices  212 us (18%)
  matrix products  122 us (11%)
  local copies, waits for them, and re-layouts  117 us (10%)
  blocking collectives  97.4 us (8%)
  starting transfers between devices  12.2 us (1%)
    another operation x48, other arithmetic, body(): lower_factor = jnp.linalg.cholesky(gram_matrix)  462 us
    all_to_all x2, waiting for transfers between devices, route_products(): lax.all_to_all(outgoing, 'sec', split_axis=0, concat_axis=0, tiled=True)  183 us
    all_to_all x1, blocking collectives, route_products(): lax.all_to_all(outgoing, 'sec', split_axis=0, concat_axis=0, tiled=True)  97.4 us
    another operation x2, other arithmetic, body(): lax.linalg.triangular_solve(lower_factor, stacked.astype(jnp.float32), le...  79.6 us
    unnamed x26, local copies, waits for them, and re-layouts  69.2 us
    dot_general x3, matrix products, pick_blocks(): jnp.dot(pick_map, received, preferred_element_type=jnp.float32)  30.3 us
    ppermute x2, waiting for transfers between devices, from_behind(): lax.ppermute(shard, axis, [(i, (i + by) % size) for i in range(size)])  28.4 us
    another operation x7, matrix products, body(): lax.linalg.triangular_solve(lower_factor, stacked.astype(jnp.float32), le...  24.9 us
  transfers between devices with their start and end apart: 4, of which 4 were waited for; matrix products, arithmetic and copies ran while one was open for 0% of the time, Pallas kernels for 0%

commit v1 on v0

v1 whole, which is shorter than its diff:
```python
import functools
import math

import jax
import jax.numpy as jnp
from jax import lax
from jax.experimental import pallas as pl
from jax.experimental.pallas import tpu as pltpu
from jax.sharding import PartitionSpec as P

ROUNDS = 3
TILE = 128
SUB = 8
HIGH = lax.Precision.HIGHEST


def from_behind(shard, axis, by):
    size = lax.axis_size(axis)
    return lax.ppermute(shard, axis, [(i, (i + by) % size) for i in range(size)])


def products_kernel(target_ref, factor_ref, block_ref, out_ref):
    out_ref[0] = jnp.dot(
        factor_ref[0].astype(jnp.bfloat16), block_ref[0], preferred_element_type=jnp.float32
    ).astype(jnp.bfloat16)


def products_by_target(factor, blocks, target, groups):
    count, size = blocks.shape[0], blocks.shape[-1]
    phys_count = count // factor.shape[0]
    return pl.pallas_call(
        products_kernel,
        out_shape=jax.ShapeDtypeStruct((groups, size, size), jnp.bfloat16),
        grid_spec=pltpu.PrefetchScalarGridSpec(
            num_scalar_prefetch=1,
            grid=(count,),
            in_specs=[
                pl.BlockSpec((1, size, size), lambda g, t: (g // phys_count, 0, 0)),
                pl.BlockSpec((1, size, size), lambda g, t: (g, 0, 0)),
            ],
            out_specs=pl.BlockSpec((1, size, size), lambda g, t: (t[g], 0, 0)),
        ),
        compiler_params=pltpu.CompilerParams(vmem_limit_bytes=32 * 2**20),
    )(target, factor, blocks)


def eliminate(sectors):
    groups = TILE // SUB
    lane = lax.broadcasted_iota(jnp.int32, (SUB, TILE), 1)
    sub = lax.broadcasted_iota(jnp.int32, (SUB, TILE), 0)
    for q in range(groups):
        base = q * SUB
        spread = [
            {
                g: [
                    jnp.broadcast_to(rows[g][:, base + j : base + j + 1], (SUB, TILE))
                    for j in range(SUB)
                ]
                for g in range(q, groups)
            }
            for rows in sectors
        ]
        for j in range(SUB):
            here = lane == base + j
            below = sub > j
            for rows, columns in zip(sectors, spread):
                top = columns[q]
                inverse = 1.0 / jnp.broadcast_to(top[j][j : j + 1, :], (SUB, TILE))
                pivot_row = jnp.broadcast_to(rows[q][j : j + 1, :], (SUB, TILE))
                pivot_row = jnp.where(here, 1.0, pivot_row) * inverse
                ahead = [
                    jnp.broadcast_to(top[m][j : j + 1, :], (SUB, TILE)) * inverse
                    for m in range(j + 1, SUB)
                ]
                for g in range(q, groups):
                    column = columns[g][j]
                    clear = here
                    if g == q:
                        column = jnp.where(below, column, 0.0)
                        clear = here & below
                    rows[g] = jnp.where(clear, 0.0, rows[g]) - column * pivot_row
                    for m in range(j + 1, SUB):
                        columns[g][m] = columns[g][m] - column * ahead[m - j - 1]


def factor_kernel(last, phys_count, idx_ref, width_ref, recv_ref, *refs):
    if last:
        upper_ref, iso_ref, work, head, rest, lead, tail = refs
    else:
        upper_ref, work, head, rest = refs
    sec_local, size = work.shape[0], work.shape[1]
    steps = size // TILE

    def add_gram(t, _):
        b = t // phys_count
        x = recv_ref[idx_ref[t]]
        part = lax.dot_general(
            x, x, (((0,), (0,)), ((), ())), preferred_element_type=jnp.float32
        )

        @pl.when(t % phys_count == 0)
        def _():
            r = lax.broadcasted_iota(jnp.int32, (size, size), 0)
            c = lax.broadcasted_iota(jnp.int32, (size, size), 1)
            work[b] = part + jnp.where((r == c) & (c >= width_ref[b]), 1.0, 0.0)

        @pl.when(t % phys_count != 0)
        def _():
            work[b] = work[b] + part

        return 0

    lax.fori_loop(0, sec_local * phys_count, add_gram, 0)
    lane = lax.broadcasted_iota(jnp.int32, (SUB, TILE), 1)
    sub = lax.broadcasted_iota(jnp.int32, (SUB, TILE), 0)
    block_of_lane = lax.broadcasted_iota(jnp.int32, (TILE, size), 1) // TILE

    def step(k, _):
        at = pl.ds(pl.multiple_of(k * TILE, TILE), TILE)
        sectors = [
            [
                work[b, pl.ds(pl.multiple_of(k * TILE + SUB * g, SUB), SUB), at]
                for g in range(TILE // SUB)
            ]
            for b in range(sec_local)
        ]
        eliminate(sectors)
        for b in range(sec_local):
            for g in range(TILE // SUB):
                m = sectors[b][g]
                row = sub + SUB * g
                diag = jnp.sum(jnp.where(lane == row, m, 0.0), axis=1, keepdims=True)
                scale = jnp.broadcast_to(lax.rsqrt(diag), (SUB, TILE))
                at_g = pl.ds(SUB * g, SUB)
                head[b, at_g, :] = jnp.where(lane >= row, m, 0.0) * scale
                rest[b, at_g, :] = jnp.where(
                    lane < row, m, jnp.where(lane == row, 1.0, 0.0)
                ) * scale
        for b in range(sec_local):
            row = jnp.dot(
                rest[b], work[b, at, :], precision=HIGH, preferred_element_type=jnp.float32
            )
            work[b, at, :] = row
            work[b, at, at] = rest[b]
            upper_ref[b, at, :] = jnp.where(block_of_lane > k, row, 0.0).astype(upper_ref.dtype)
            upper_ref[b, at, at] = head[b].astype(upper_ref.dtype)
        for i in range(1, steps):

            @pl.when(i > k)
            def _():
                mine = pl.ds(i * TILE, TILE)
                for b in range(sec_local):
                    work[b, mine, at] = jnp.zeros((TILE, TILE), jnp.float32)
                    work[b, mine, :] = work[b, mine, :] - lax.dot_general(
                        work[b, at, mine],
                        work[b, at, :],
                        (((0,), (0,)), ((), ())),
                        precision=HIGH,
                        preferred_element_type=jnp.float32,
                    )

        return 0

    lax.fori_loop(0, steps, step, 0)
    if last:
        scale = math.sqrt(phys_count * size)
        for b in range(sec_local):
            for i in range(steps):
                mine = pl.ds(i * TILE, TILE)
                w = jnp.where(block_of_lane <= i, work[b, mine, :], 0.0) * scale
                hi = w.astype(jnp.bfloat16)
                lead[b, mine, :] = hi
                tail[b, mine, :] = (w - hi.astype(jnp.float32)).astype(jnp.bfloat16)

        def apply(t, _):
            b = t // phys_count
            x = recv_ref[idx_ref[t]]
            dims = (((1,), (1,)), ((), ()))
            iso_ref[t] = lax.dot_general(
                x, lead[b], dims, preferred_element_type=jnp.float32
            ) + lax.dot_general(x, tail[b], dims, preferred_element_type=jnp.float32)
            return 0

        lax.fori_loop(0, sec_local * phys_count, apply, 0)


def factorise(received, index, widths, sec_local, phys_count, last):
    size = received.shape[-1]
    vmem = pl.BlockSpec(memory_space=pltpu.VMEM)
    smem = pl.BlockSpec(memory_space=pltpu.SMEM)
    full = (sec_local, size, size)
    out_shape = [jax.ShapeDtypeStruct(full, jnp.float32 if last else jnp.bfloat16)]
    scratch = [
        pltpu.VMEM(full, jnp.float32),
        pltpu.VMEM((sec_local, TILE, TILE), jnp.float32),
        pltpu.VMEM((sec_local, TILE, TILE), jnp.float32),
    ]
    if last:
        out_shape.append(
            jax.ShapeDtypeStruct((sec_local * phys_count, size, size), jnp.float32)
        )
        scratch += [pltpu.VMEM(full, jnp.bfloat16)] * 2
    return pl.pallas_call(
        functools.partial(factor_kernel, last, phys_count),
        out_shape=out_shape,
        in_specs=[smem, smem, vmem],
        out_specs=[vmem] * len(out_shape),
        scratch_shapes=scratch,
        compiler_params=pltpu.CompilerParams(vmem_limit_bytes=48 * 2**20),
    )(index, widths, received)


def body(tensors, factors, sector_sizes, merging):
    site_index = lax.axis_index("site")
    sec_index = lax.axis_index("sec")
    site_count = lax.axis_size("site")
    sec_groups = lax.axis_size("sec")
    blocks = tensors[0]
    sec_local, phys_count, size = (blocks.shape[0], blocks.shape[1], blocks.shape[3])
    local_count = sec_local * phys_count
    blocks = blocks.reshape(local_count, size, size)
    rows = lax.dynamic_index_in_dim(merging, site_index, 0, keepdims=False)
    next_widths = lax.dynamic_index_in_dim(
        sector_sizes, (site_index + 1) % site_count, 0, keepdims=False
    )
    widths = lax.dynamic_slice_in_dim(next_widths, sec_index * sec_local, sec_local)
    own = lax.dynamic_slice_in_dim(rows, sec_index * sec_local, sec_local)
    target = own.reshape(local_count) // sec_local
    wanted = sec_index * sec_local + jnp.arange(sec_local, dtype=jnp.int32)
    match = (rows[None] == wanted[:, None, None]).astype(jnp.int32)
    left = jnp.arange(rows.shape[0], dtype=jnp.int32) // sec_local
    index = jnp.sum(match * left[None, :, None], axis=1).reshape(local_count)
    carried = factors[0]
    for step_index in range(ROUNDS):
        last = step_index + 1 == ROUNDS
        outgoing = products_by_target(carried, blocks, target, sec_groups)
        received = lax.all_to_all(outgoing, "sec", split_axis=0, concat_axis=0, tiled=True)
        out = factorise(received, index, widths, sec_local, phys_count, last)
        if not last:
            carried = from_behind(out[0], "site", 1)
    upper, isometry = out
    return (isometry.reshape(1, sec_local, phys_count, size, size), upper[None])


def solution(mesh):
    in_specs = (P("site", "sec", None, None, None), P("site", "sec", None, None), P(), P())
    out_specs = (P("site", "sec", None, None, None), P("site", "sec", None, None))
    return jax.shard_map(body, mesh=mesh, in_specs=in_specs, out_specs=out_specs, check_vma=False)
```

time: 1150 us -> 480 us (0.42)
  other arithmetic: 583 us -> 0.23 us
  Pallas kernels: 0 us -> 152 us
  matrix products: 122 us -> 0 us
  local copies, waits for them, and re-layouts: 117 us -> 7.58 us
  blocking collectives: 97.4 us -> 191 us
  waiting for transfers between devices: 212 us -> 121 us
    another operation x50 -> x0, other arithmetic: 542 us -> none  [the longest x48 462 us: body(): lower_factor = jnp.linalg.cholesky(gram_matrix)]
    pallas_call x0 -> x6, Pallas kernels: none -> 152 us  [the longest x3 140 us: factorise(): pl.pallas_call(functools.partial(factor_kernel, last, phys_count), out_sh...]
    all_to_all x1 -> x2, blocking collectives: 97.4 us -> 191 us  [body(): lax.all_to_all(outgoing, 'sec', split_axis=0, concat_axis=0, tiled=True)]
    all_to_all x2 -> x1, waiting for transfers between devices: 183 us -> 92.2 us  [body(): lax.all_to_all(outgoing, 'sec', split_axis=0, concat_axis=0, tiled=True)]
    dot_general x13 -> x0, matrix products: 77 us -> none  [the longest x3 30.3 us: pick_blocks(): jnp.dot(pick_map, received, preferred_element_type=jnp.float32)]
    unnamed x26 -> x10, local copies, waits for them, and re-layouts: 69.2 us -> 6.47 us
    another operation x25 -> x0, matrix products: 45.1 us -> none  [the longest x7 24.9 us: body(): lax.linalg.triangular_solve(lower_factor, stacked.astype(jnp.float32), le...]
    all_to_all x3 -> x0, other arithmetic: 19.7 us -> none  [route_products(): lax.all_to_all(outgoing, 'sec', split_axis=0, concat_axis=0, tiled=True)]
  transfers between devices with their start and end apart: 4 -> 3, of which waited for: 4 -> 3; matrix products, arithmetic and copies ran while one was open for 0% -> 0% of each run, Pallas kernels for 0% -> 0%
where the time goes in v1:
time: 480 us
  blocking collectives  191 us (40%)
  Pallas kernels  152 us (32%)
  waiting for transfers between devices  121 us (25%)
  local copies, waits for them, and re-layouts  7.58 us (2%)
  starting transfers between devices  7.4 us (2%)
    all_to_all x2, blocking collectives, body(): lax.all_to_all(outgoing, 'sec', split_axis=0, concat_axis=0, tiled=True)  191 us
    pallas_call x3, Pallas kernels, factorise(): pl.pallas_call(functools.partial(factor_kernel, last, phys_count), out_sh...  140 us
    all_to_all x1, waiting for transfers between devices, body(): lax.all_to_all(outgoing, 'sec', split_axis=0, concat_axis=0, tiled=True)  92.2 us
    ppermute x2, waiting for transfers between devices, from_behind(): lax.ppermute(shard, axis, [(i, (i + by) % size) for i in range(size)])  28.4 us
    pallas_call x3, Pallas kernels, products_by_target(): pl.pallas_call(products_kernel, out_shape=jax.ShapeDtypeStruct((groups, s...  12.4 us
  transfers between devices with their start and end apart: 3, of which 3 were waited for; matrix products, arithmetic and copies ran while one was open for 0% of the time, Pallas kernels for 0%

profile of v1, /device:TPU:0, one launch (start us, length us, event | category | flops | bytes accessed | tf_op | source)
XLA Modules:
  0.0 479.6 jit_solution(4437562830250404378)
XLA Ops:
  0.6 0.0 copy-start
  0.7 0.7 copy-done
  1.3 0.1 constant_dynamic-slice_fusion
  1.4 0.1 copy.8
  1.5 0.1 reshape.34
  1.6 0.0 copy-start.1
  1.6 2.2 copy-done.1
  3.8 0.0 copy-start.4
  3.8 1.6 copy-done.4
  5.4 4.1 shard_map.59
  9.5 0.0 copy-start.3
  9.5 2.0 copy-done.3
  11.5 7.3 %all-to-all-start = ((bf16[8,512,512]{2,1,0:T(8,128)(2,1)}), bf16[8,512,512]{2,1,0:T(8,128)(2,1)}, u32[]{:S(2)}, u32[]{:S(2)}) async-start(bf16[8,512,512]{2,1,0:T(8,128)(2,1)} %copy-done.3), calls=%async_computation | async-start | bytes 8388608 | tf_op jit(solution)/shard_map/all_to_all | solution.py:237
  18.9 0.2 select_reduce_fusion
  19.1 0.1 reshape.33.idx_ref
  19.1 0.8 dynamic-slice_bitcast_fusion.1.width_ref
  19.9 92.2 %all-to-all-done.recv_ref = bf16[8,512,512]{2,1,0:T(8,128)(2,1)} async-done(((bf16[8,512,512]{2,1,0:T(8,128)(2,1)}), bf16[8,512,512]{2,1,0:T(8,128)(2,1)}, u32[]{:S(2)}, u32[]{:S(2)}) %all-to-all-start) | async-done | bytes 4194336 | tf_op jit(solution)/shard_map/all_to_all | solution.py:237
  112.1 0.0 copy-start.2
  112.1 44.6 %shard_map.60 = bf16[2,512,512]{2,1,0:T(8,128)(2,1)S(1)} custom-call(s32[8]{0:T(128)S(1)} %reshape.33.idx_ref, s32[2]{0:T(128)S(1)} %dynamic-slice_bitcast_fusion.1.width_ref, bf16[8,512,512]{2,1,0:T(8,128)(2,1)} %all-to-all-done.recv_ref), custom_call_target="tpu_custom_call" | custom-call | tf_op jit(solution)/shard_map/pallas_call | solution.py:203
  156.7 0.1 collective-permute-start
  156.8 14.2 %collective-permute-done.factor_ref = bf16[2,512,512]{2,1,0:T(8,128)(2,1)S(1)} collective-permute-done((bf16[2,512,512]{2,1,0:T(8,128)(2,1)S(1)}, bf16[2,512,512]{2,1,0:T(8,128)(2,1)S(1)}, u32[]{:S(2)}, u32[]{:S(2)}) %collective-permute-start) | collective-permute-done | bytes 1048608 | tf_op jit(solution)/shard_map/ppermute | solution.py:19
  171.0 0.0 copy-done.2
  171.0 4.1 shard_map.61
  175.1 96.1 %all_to_all.15.recv_ref = bf16[8,512,512]{2,1,0:T(8,128)(2,1)S(1)} all-to-all(bf16[8,512,512]{2,1,0:T(8,128)(2,1)S(1)} %shard_map.61), channel_id=1, replica_groups=mesh['site'=4,'sec'=8] {'sec'}, dimensions={0} | all-to-all | bytes 8388608 | tf_op jit(solution)/shard_map/all_to_all | solution.py:237
  271.3 42.8 %shard_map.62 = bf16[2,512,512]{2,1,0:T(8,128)(2,1)S(1)} custom-call(s32[8]{0:T(128)S(1)} %reshape.33.idx_ref, s32[2]{0:T(128)S(1)} %dynamic-slice_bitcast_fusion.1.width_ref, bf16[8,512,512]{2,1,0:T(8,128)(2,1)S(1)} %all_to_all.15.recv_ref), custom_call_target="tpu_custom_call" | custom-call | tf_op jit(solution)/shard_map/pallas_call | solution.py:203
  314.1 0.1 collective-permute-start.1
  314.2 14.2 %collective-permute-done.1.factor_ref = bf16[2,512,512]{2,1,0:T(8,128)(2,1)S(1)} collective-permute-done((bf16[2,512,512]{2,1,0:T(8,128)(2,1)S(1)}, bf16[2,512,512]{2,1,0:T(8,128)(2,1)S(1)}, u32[]{:S(2)}, u32[]{:S(2)}) %collective-permute-start.1) | collective-permute-done | bytes 1048608 | tf_op jit(solution)/shard_map/ppermute | solution.py:19
  328.4 4.1 shard_map.63
  332.5 94.7 %all_to_all.16.recv_ref = bf16[8,512,512]{2,1,0:T(8,128)(2,1)S(1)} all-to-all(bf16[8,512,512]{2,1,0:T(8,128)(2,1)S(1)} %shard_map.63), channel_id=1, replica_groups=mesh['site'=4,'sec'=8] {'sec'}, dimensions={0} | all-to-all | bytes 8388608 | tf_op jit(solution)/shard_map/all_to_all | solution.py:237
  427.2 52.4 %shard_map.64 = (f32[2,512,512]{2,1,0:T(8,128)}, f32[8,512,512]{2,1,0:T(8,128)}) custom-call(s32[8]{0:T(128)S(1)} %reshape.33.idx_ref, s32[2]{0:T(128)S(1)} %dynamic-slice_bitcast_fusion.1.width_ref, bf16[8,512,512]{2,1,0:T(8,128)(2,1)S(1)} %all_to_all.16.recv_ref), custom_call_target="tpu_custom_call" | custom-call | tf_op jit(solution)/shard_map/pallas_call | solution.py:203
  (4 shorter events, 0.0 us)
Async XLA Ops:
  0.6 0.7 copy-start
  1.6 2.2 copy-start.1
  3.8 1.6 copy-start.4
  9.5 2.0 copy-start.3
  11.5 100.6 %all-to-all-start = ((bf16[8,512,512]{2,1,0:T(8,128)(2,1)}), bf16[8,512,512]{2,1,0:T(8,128)(2,1)}, u32[]{:S(2)}, u32[]{:S(2)}) async-start(bf16[8,512,512]{2,1,0:T(8,128)(2,1)} %copy-done.3), calls=%async_computation | async-start | bytes 8388608 | tf_op jit(solution)/shard_map/all_to_all | solution.py:237
  112.1 58.9 %copy-start.2 = (bf16[1,2,4,512,512]{4,3,2,1,0:T(8,128)(2,1)S(1)}, bf16[1,2,4,512,512]{4,3,2,1,0:T(8,128)(2,1)}, u32[]{:S(2)}) copy-start(bf16[1,2,4,512,512]{4,3,2,1,0:T(8,128)(2,1)} %param.4) | copy-start | bytes 12582916
  156.7 14.3 %collective-permute-start = (bf16[2,512,512]{2,1,0:T(8,128)(2,1)S(1)}, bf16[2,512,512]{2,1,0:T(8,128)(2,1)S(1)}, u32[]{:S(2)}, u32[]{:S(2)}) collective-permute-start(bf16[2,512,512]{2,1,0:T(8,128)(2,1)S(1)} %shard_map.60), channel_id=1, source_target_pairs={{0,8},{8,16},{16,24},{24,0},{1,9},{9,17},{17,25},{25,1},{2,10},{10... | collective-permute-start | bytes 3145736 | tf_op jit(solution)/shard_map/ppermute | solution.py:19
  314.1 14.3 %collective-permute-start.1 = (bf16[2,512,512]{2,1,0:T(8,128)(2,1)S(1)}, bf16[2,512,512]{2,1,0:T(8,128)(2,1)S(1)}, u32[]{:S(2)}, u32[]{:S(2)}) collective-permute-start(bf16[2,512,512]{2,1,0:T(8,128)(2,1)S(1)} %shard_map.62), channel_id=1, source_target_pairs={{0,8},{8,16},{16,24},{24,0},{1,9},{9,17},{17,25},{25,1},{2,10},{10... | collective-permute-start | bytes 3145736 | tf_op jit(solution)/shard_map/ppermute | solution.py:19
